TPU v7x, 32 devices: a whole 2x2x4 slice. The times are simulated.
32 devices in a mesh: gx: 8 (over y, x, core), yz: 4 (over z).
Axes of the slice: x: 2, y: 2, z: 4, core: 2. Of those that a mesh axis runs over, the one named last changes fastest.
Arguments:
- vectors: float32 [8, 128, 64, 512], P(None, 'gx', 'yz'), may hold values from -4 to 4
- classes: int32 [128, 64, 512], P('gx', 'yz'), may hold values from 0 to 3
- permittivity: float32 [4], replicated, may hold values from 0.01 to 10
Outputs:
- applied: float32 [8, 128, 64, 512], P(None, 'gx', 'yz')
- coarse: float32 [256, 256], P('gx', 'yz')
All inputs are finite; a program needn't handle non-finite values.
Results may differ from a plain program's by a relative error of at most 0.000071.
Values sent between devices are 32-bit elements; how exact they have to be, the bound alone decides.
A program may use at most 64 MiB of HBM per device.

v0:
```python
import jax
import jax.numpy as jnp
from jax import lax
from jax.sharding import PartitionSpec as P


def padded_2(block, sides, width):
    for axis, dim in sides:
        count = lax.axis_size(axis)
        forward = [(i, i + 1) for i in range(count - 1)]
        backward = [(target, source) for source, target in forward]
        low = lax.ppermute(
            lax.slice_in_dim(block, block.shape[dim] - width, None, axis=dim), axis, forward
        )
        high = lax.ppermute(lax.slice_in_dim(block, 0, width, axis=dim), axis, backward)
        block = jnp.concatenate([low, block, high], axis=dim)
    return block


def permit(classes, permittivity):
    onehot = (classes[..., None] == jnp.arange(permittivity.shape[0], dtype=jnp.int32)).astype(
        jnp.float32
    )
    return jnp.sum(onehot * permittivity, axis=-1)


def harmonic(first_value, second_value):
    return 2.0 * first_value * second_value / (first_value + second_value)


def stencil(vectors, epsilon, x_low, x_high, z_low, z_high):
    full_x = jnp.concatenate([x_low, epsilon, x_high], axis=0)
    face_x = harmonic(full_x[:-1], full_x[1:])
    pad_x = jnp.pad(vectors, ((0, 0), (1, 1), (0, 0), (0, 0)))
    applied = face_x[:-1] * (vectors - pad_x[:, :-2]) + face_x[1:] * (vectors - pad_x[:, 2:])
    full_z = jnp.concatenate([z_low, epsilon, z_high], axis=1)
    face_z = harmonic(full_z[:, :-1], full_z[:, 1:])
    pad_z = jnp.pad(vectors, ((0, 0), (0, 0), (1, 1), (0, 0)))
    applied = (
        applied
        + face_z[:, :-1] * (vectors - pad_z[:, :, :-2])
        + face_z[:, 1:] * (vectors - pad_z[:, :, 2:])
    )
    face_y = jnp.pad(harmonic(epsilon[..., :-1], epsilon[..., 1:]), ((0, 0), (0, 0), (1, 1)))
    pad_y = jnp.pad(vectors, ((0, 0), (0, 0), (0, 0), (1, 1)))
    applied = (
        applied
        + face_y[..., :-1] * (vectors - pad_y[..., :-2])
        + face_y[..., 1:] * (vectors - pad_y[..., 2:])
    )
    return applied


def coupling(own_face, own_eps, other_face, other_eps):
    weighted = own_face * harmonic(own_eps, other_eps)
    return -jnp.einsum("kzy,lzy->kl", weighted, other_face, precision=lax.Precision.HIGHEST)


def place_blocks(blocks, targets, first_column, width):
    local = targets - first_column
    onehot = (local[..., None] == jnp.arange(width, dtype=jnp.int32)).astype(jnp.float32)
    placed = jnp.einsum("rmkl,rms->rksl", blocks, onehot, precision=lax.Precision.HIGHEST)
    return placed.reshape(blocks.shape[0] * blocks.shape[2], width * blocks.shape[3])


def shards(vectors, classes, permittivity):
    vector_count = vectors.shape[0]
    epsilon = permit(classes, permittivity)
    stacked = jnp.concatenate([vectors, epsilon[None]], axis=0)
    padded = padded_2(stacked, (("gx", 1), ("yz", 2)), 1)
    x_low = padded[:, 0, 1:-1]
    x_high = padded[:, -1, 1:-1]
    z_low = padded[:, 1:-1, 0]
    z_high = padded[:, 1:-1, -1]
    applied = stencil(
        vectors,
        epsilon,
        x_low[vector_count][None],
        x_high[vector_count][None],
        z_low[vector_count][:, None],
        z_high[vector_count][:, None],
    )
    upper_x = coupling(vectors[:, -1], epsilon[-1], x_high[:vector_count], x_high[vector_count])
    lower_x = coupling(vectors[:, 0], epsilon[0], x_low[:vector_count], x_low[vector_count])
    upper_z = coupling(
        vectors[:, :, -1], epsilon[:, -1], z_high[:vector_count], z_high[vector_count]
    )
    lower_z = coupling(vectors[:, :, 0], epsilon[:, 0], z_low[:vector_count], z_low[vector_count])
    self_block = jnp.einsum("kxzy,lxzy->kl", vectors, applied, precision=lax.Precision.HIGHEST)
    scaling = 1.0 / (vectors.shape[2] * vectors.shape[3])
    blocks = jnp.stack([self_block, upper_x, lower_x, upper_z, lower_z]) * scaling
    tile_count = lax.axis_size("yz")
    order_total = tile_count * lax.axis_size("gx")
    slab_index = lax.axis_index("gx")
    tile_index = lax.axis_index("yz")
    offsets = jnp.array([0, tile_count, -tile_count, 1, -1], jnp.int32)
    own_ids = slab_index * tile_count + jnp.reshape(tile_index, (1,))
    row_slab = place_blocks(
        blocks[None], jnp.mod(own_ids[:, None] + offsets, order_total), 0, order_total
    )
    coarse = lax.all_to_all(row_slab, "yz", split_axis=1, concat_axis=0, tiled=True)
    return (applied, coarse)


def solution(mesh):
    return jax.shard_map(
        shards,
        mesh=mesh,
        in_specs=(P(None, "gx", "yz", None), P("gx", "yz", None), P()),
        out_specs=(P(None, "gx", "yz", None), P("gx", "yz")),
        check_vma=False,
    )
```

profile of v0, /device:TPU:2, one launch (start us, length us, event | category | flops | bytes accessed | tf_op | source)
XLA Modules:
  0.0 101.1 jit_solution(11439314746042404381)
XLA Ops:
  0.6 1.4 %select_reduce_fusion = f32[16,16,512]{2,1,0:T(8,128)S(1)} fusion(f32[4]{0:T(128)} %param.6, s32[16,16,512]{2,1,0:T(8,128)} %param.5), kind=kLoop, calls=%fused_computation.27 | loop fusion | flops 1441792 | bytes 1048592 | tf_op jit(solution)/shard_map/reduce_sum | solution.py:24
  2.4 7.7 %copy_dynamic-update-slice_fusion = f32[9,16,16,512]{3,0,2,1:T(8,128)} fusion(f32[8,16,16,512]{3,2,1,0:T(8,128)} %param.4), kind=kLoop, calls=%fused_computation.26 | loop fusion | bytes 8388608
  10.1 11.4 %dynamic-update-slice.1 = f32[9,16,16,512]{3,0,2,1:T(8,128)} dynamic-update-slice(f32[9,16,16,512]{3,0,2,1:T(8,128)} %copy_dynamic-update-slice_fusion, f32[1,16,16,512]{3,0,2,1:T(1,128)S(1)} %broadcast_in_dim.2, s32[]{} %constant.55, s32[]{} %constant.54, s32[]{} %constant.54, s32[]{} %constant.54) | dynamic-update-slice | bytes 1048580 | tf_op jit(solution)/shard_map/concatenate | solution.py:69
  21.5 2.1 %fusion.48 = (f32[9,1,16,512]{3,0,2,1:T(8,128)}, f32[9,1,16,512]{3,0,2,1:T(8,128)S(1)}) fusion(f32[9,16,16,512]{3,0,2,1:T(8,128)} %dynamic-update-slice.1), kind=kLoop, calls=%fused_computation.96 | loop fusion | bytes 1179648 | tf_op jit(solution)/shard_map/slice | solution.py:13
  23.6 1.9 %collective-permute-start = (f32[9,1,16,512]{3,0,2,1:T(8,128)}, f32[9,1,16,512]{3,0,2,1:T(8,128)S(1)}, u32[]{:S(2)}, u32[]{:S(2)}) collective-permute-start(f32[9,1,16,512]{3,0,2,1:T(8,128)} %get-tuple-element.4), channel_id=1, source_target_pairs={{0,4},{4,8},{8,12},{12,16},{16,20},{20,24},{24,28},{1,5},{5,9},{9,... | collective-permute-start | bytes 884744 | tf_op jit(solution)/shard_map/ppermute | solution.py:12
  25.5 3.6 %collective-permute-start.1 = (f32[9,1,16,512]{3,0,2,1:T(8,128)S(1)}, f32[9,1,16,512]{3,0,2,1:T(8,128)S(1)}, u32[]{:S(2)}, u32[]{:S(2)}) collective-permute-start(f32[9,1,16,512]{3,0,2,1:T(8,128)S(1)} %get-tuple-element.5), channel_id=1, source_target_pairs={{4,0},{8,4},{12,8},{16,12},{20,16},{24,20},{28,24},{5,1},{9,5},{13... | collective-permute-start | bytes 884744 | tf_op jit(solution)/shard_map/ppermute | solution.py:15
  29.5 3.5 %fusion.49 = (f32[8,16,1,512]{3,2,1,0:T(1,128)S(1)}, f32[8,16,1,512]{3,2,1,0:T(1,128)}) fusion(f32[8,16,16,512]{3,2,1,0:T(8,128)} %param.4), kind=kLoop, calls=%fused_computation.97 | loop fusion | bytes 1048576 | tf_op jit(solution)/shard_map/slice | solution.py:88
  32.9 1.3 %collective-permute-done = f32[9,1,16,512]{3,0,2,1:T(8,128)S(1)} collective-permute-done((f32[9,1,16,512]{3,0,2,1:T(8,128)}, f32[9,1,16,512]{3,0,2,1:T(8,128)S(1)}, u32[]{:S(2)}, u32[]{:S(2)}) %collective-permute-start) | collective-permute-done | bytes 294944 | tf_op jit(solution)/shard_map/ppermute | solution.py:12
  34.3 4.6 %collective-permute-done.1 = f32[9,1,16,512]{3,0,2,1:T(8,128)S(1)} collective-permute-done((f32[9,1,16,512]{3,0,2,1:T(8,128)S(1)}, f32[9,1,16,512]{3,0,2,1:T(8,128)S(1)}, u32[]{:S(2)}, u32[]{:S(2)}) %collective-permute-start.1) | collective-permute-done | bytes 294944 | tf_op jit(solution)/shard_map/ppermute | solution.py:15
  38.9 2.2 %pad_maximum_fusion.4 = (f32[9,18,1,512]{3,0,2,1:T(8,128)S(1)}, f32[9,18,1,512]{3,0,2,1:T(8,128)}) fusion(f32[9,1,16,512]{3,0,2,1:T(8,128)S(1)} %collective-permute-done.1, f32[9,16,16,512]{3,0,2,1:T(8,128)} %dynamic-update-slice.1, f32[9,1,16,512]{3,0,2,1:T(8,128)S(1)} %collective-permute-done), kind=kLoop, calls=%fused_computation.50 | loop fusion | flops 331776 | bytes 5971968 | tf_op jit(solution)/shard_map/slice | solution.py:13
  41.1 1.0 copy.137
  42.0 4.3 %collective-permute-start.2 = (f32[9,18,1,512]{3,1,2,0:T(8,128)}, f32[9,18,1,512]{3,1,2,0:T(8,128)}, u32[]{:S(2)}, u32[]{:S(2)}) collective-permute-start(f32[9,18,1,512]{3,1,2,0:T(8,128)} %copy.137), channel_id=1, source_target_pairs={{0,1},{1,2},{2,3},{4,5},{5,6},{6,7},{8,9},{9,10},{10,11},{12,13},{... | collective-permute-start | bytes 995336 | tf_op jit(solution)/shard_map/ppermute | solution.py:12
  46.3 1.3 %collective-permute-start.3 = (f32[9,18,1,512]{3,0,2,1:T(8,128)}, f32[9,18,1,512]{3,0,2,1:T(8,128)}, u32[]{:S(2)}, u32[]{:S(2)}) collective-permute-start(f32[9,18,1,512]{3,0,2,1:T(8,128)} %get-tuple-element.3), channel_id=1, source_target_pairs={{1,0},{2,1},{3,2},{5,4},{6,5},{7,6},{9,8},{10,9},{11,10},{13,12},{... | collective-permute-start | bytes 995336 | tf_op jit(solution)/shard_map/ppermute | solution.py:15
  47.8 1.1 %bitcast_multiply_fusion = (f32[8,16,512]{2,1,0:T(8,128)S(1)}, f32[8,16,512]{2,1,0:T(8,128)S(1)}) fusion(f32[8,16,16,512]{3,2,1,0:T(8,128)} %param.4, f32[16,512]{1,0:T(8,128)S(1)} %bitcast.123, f32[16,512]{1,0:T(8,128)S(1)} %bitcast.124), kind=kLoop, calls=%fused_computation.63 | loop fusion | flops 131072 | bytes 1114112 | tf_op jit(solution)/shard_map/mul | solution.py:55
  51.5 4.0 %collective-permute-done.2 = f32[9,18,1,512]{3,1,2,0:T(8,128)} collective-permute-done((f32[9,18,1,512]{3,1,2,0:T(8,128)}, f32[9,18,1,512]{3,1,2,0:T(8,128)}, u32[]{:S(2)}, u32[]{:S(2)}) %collective-permute-start.2) | collective-permute-done | bytes 331808 | tf_op jit(solution)/shard_map/ppermute | solution.py:12
  56.4 7.8 %collective-permute-done.3 = f32[9,18,1,512]{3,0,2,1:T(8,128)} collective-permute-done((f32[9,18,1,512]{3,0,2,1:T(8,128)}, f32[9,18,1,512]{3,0,2,1:T(8,128)}, u32[]{:S(2)}, u32[]{:S(2)}) %collective-permute-start.3) | collective-permute-done | bytes 331808 | tf_op jit(solution)/shard_map/ppermute | solution.py:15
  64.2 1.0 fusion.51
  65.8 5.8 %fusion.6 = f32[8,16,16,512]{3,2,1,0:T(8,128)S(1)} fusion(f32[8,16,16,512]{3,2,1,0:T(8,128)S(1)} %copy-done, f32[16,16,512]{2,1,0:T(8,128)S(1)} %get-tuple-element.21, f32[16,16,512]{2,1,0:T(8,128)S(1)} %get-tuple-element.20, f32[16,16,512]{2,1,0:T(8,128)S(1)} %get-tuple-element.22, f32[16,16,512]{2,1,0:T(8,128)S(1)} %get-tuple-element.23, ...), kind=kLoop, calls=%fused_computation.12 | loop fusion | flops 17825792 | bytes 11534336 | tf_op jit(solution)/shard_map/add | solution.py:47
  71.6 2.0 %copy-done.1 = f32[8,16,16,512]{3,2,1,0:T(8,128)} copy-done((f32[8,16,16,512]{3,2,1,0:T(8,128)}, f32[8,16,16,512]{3,2,1,0:T(8,128)S(1)}, u32[]{:S(2)}) %copy-start.1) | copy-done | bytes 4194328
  73.6 11.7 %fusion.20 = f32[1,8,8]{1,2,0:T(8,128)S(1)} fusion(f32[8,16,16,512]{3,2,1,0:T(8,128)S(1)} %copy-done, f32[8,16,16,512]{3,2,1,0:T(8,128)S(1)} %fusion.6), kind=kOutput, calls=%fused_computation.30 | convolution fusion | flops 100663296 | bytes 8388864 | tf_op jit(solution)/shard_map/kxzy,lxzy->kl/dot_general | solution.py:89
  86.3 1.0 %slice_bitcast_fusion = f32[8,16,512]{2,1,0:T(8,128)S(1)} fusion(f32[9,18,1,512]{3,1,2,0:T(8,128)} %collective-permute-done.2), kind=kLoop, calls=%fused_computation.55 | loop fusion | bytes 524288 | tf_op jit(solution)/shard_map/slice | solution.py:88
  87.4 0.9 fusion.26
  88.4 1.7 %fusion.28 = f32[1,8,8]{2,1,0:T(8,128)S(1)} fusion(f32[9,18,1,512]{3,0,2,1:T(8,128)} %collective-permute-done.3, f32[8,16,512]{2,1,0:T(8,128)S(1)} %get-tuple-element.25), kind=kOutput, calls=%fused_computation.36 | convolution fusion | flops 6291520 | bytes 524544 | tf_op jit(solution)/shard_map/kzy,lzy->kl/dot_general | solution.py:56
  90.8 8.5 %all_to_all.19 = f32[4,1,512]{2,1,0:T(1,128)S(1)} all-to-all(f32[4,1,512]{2,1,0:T(1,128)S(1)} %reshape.130), channel_id=1, replica_groups=mesh['gx'=8,'yz'=4] {'yz'}, dimensions={0} | all-to-all | bytes 16384 | tf_op jit(solution)/shard_map/all_to_all | solution.py:101
  (46 shorter events, 8.6 us)
Async XLA Ops:
  10.1 19.3 %copy-start.3 = (s32[5]{0:T(128)S(1)}, s32[5]{0:T(128)}, u32[]{:S(2)}) copy-start(s32[5]{0:T(128)} %constant.40.clone) | copy-start | bytes 64
  23.6 10.7 %collective-permute-start = (f32[9,1,16,512]{3,0,2,1:T(8,128)}, f32[9,1,16,512]{3,0,2,1:T(8,128)S(1)}, u32[]{:S(2)}, u32[]{:S(2)}) collective-permute-start(f32[9,1,16,512]{3,0,2,1:T(8,128)} %get-tuple-element.4), channel_id=1, source_target_pairs={{0,4},{4,8},{8,12},{12,16},{16,20},{20,24},{24,28},{1,5},{5,9},{9,... | collective-permute-start | bytes 884744 | tf_op jit(solution)/shard_map/ppermute | solution.py:12
  25.5 13.4 %collective-permute-start.1 = (f32[9,1,16,512]{3,0,2,1:T(8,128)S(1)}, f32[9,1,16,512]{3,0,2,1:T(8,128)S(1)}, u32[]{:S(2)}, u32[]{:S(2)}) collective-permute-start(f32[9,1,16,512]{3,0,2,1:T(8,128)S(1)} %get-tuple-element.5), channel_id=1, source_target_pairs={{4,0},{8,4},{12,8},{16,12},{20,16},{24,20},{28,24},{5,1},{9,5},{13... | collective-permute-start | bytes 884744 | tf_op jit(solution)/shard_map/ppermute | solution.py:15
  42.0 13.6 %collective-permute-start.2 = (f32[9,18,1,512]{3,1,2,0:T(8,128)}, f32[9,18,1,512]{3,1,2,0:T(8,128)}, u32[]{:S(2)}, u32[]{:S(2)}) collective-permute-start(f32[9,18,1,512]{3,1,2,0:T(8,128)} %copy.137), channel_id=1, source_target_pairs={{0,1},{1,2},{2,3},{4,5},{5,6},{6,7},{8,9},{9,10},{10,11},{12,13},{... | collective-permute-start | bytes 995336 | tf_op jit(solution)/shard_map/ppermute | solution.py:12
  46.3 18.0 %collective-permute-start.3 = (f32[9,18,1,512]{3,0,2,1:T(8,128)}, f32[9,18,1,512]{3,0,2,1:T(8,128)}, u32[]{:S(2)}, u32[]{:S(2)}) collective-permute-start(f32[9,18,1,512]{3,0,2,1:T(8,128)} %get-tuple-element.3), channel_id=1, source_target_pairs={{1,0},{2,1},{3,2},{5,4},{6,5},{7,6},{9,8},{10,9},{11,10},{13,12},{... | collective-permute-start | bytes 995336 | tf_op jit(solution)/shard_map/ppermute | solution.py:15
  51.5 14.2 %copy-start = (f32[8,16,16,512]{3,2,1,0:T(8,128)S(1)}, f32[8,16,16,512]{3,2,1,0:T(8,128)}, u32[]{:S(2)}) copy-start(f32[8,16,16,512]{3,2,1,0:T(8,128)} %param.4) | copy-start | bytes 12582916
  71.5 2.0 %copy-start.1 = (f32[8,16,16,512]{3,2,1,0:T(8,128)}, f32[8,16,16,512]{3,2,1,0:T(8,128)S(1)}, u32[]{:S(2)}) copy-start(f32[8,16,16,512]{3,2,1,0:T(8,128)S(1)} %fusion.6) | copy-start | bytes 12582916
  73.6 12.7 %copy-start.2 = (f32[8,16,1,512]{3,2,1,0:T(1,128)S(1)}, f32[8,16,1,512]{3,2,1,0:T(1,128)}, u32[]{:S(2)}) copy-start(f32[8,16,1,512]{3,2,1,0:T(1,128)} %get-tuple-element.7) | copy-start | bytes 786436
where the time goes:
time: 102 us; the launch traced here: 101 us
  local copies, waits for them, and re-layouts  34.4 us (34%)
  waiting for transfers between devices  17.8 us (17%)
  matrix products  15.8 us (15%)
  other arithmetic  12.6 us (12%)
  starting transfers between devices  11.1 us (11%)
  blocking collectives  8.47 us (8%)
    ppermute x2, waiting for transfers between devices, padded_2(): lax.ppermute(lax.slice_in_dim(block, 0, width, axis=dim), axis, backward)  12.4 us
    dot_general x1, matrix products, shards(): jnp.einsum('kxzy,lxzy->kl', vectors, applied, precision=lax.Precision.HIG...  11.7 us
    concatenate x1, local copies, waits for them, and re-layouts, shards(): stacked = jnp.concatenate([vectors, epsilon[None]], axis=0)  11.4 us
    unnamed x14, local copies, waits for them, and re-layouts  10.9 us
    all_to_all x1, blocking collectives, shards(): lax.all_to_all(row_slab, 'yz', split_axis=1, concat_axis=0, tiled=True)  8.47 us
    ppermute x2, starting transfers between devices, padded_2(): lax.ppermute(lax.slice_in_dim(block, block.shape[dim] - width, None, axis...  6.17 us
    add x1, other arithmetic, stencil(): applied + face_y[..., :-1] * (vectors - pad_y[..., :-2])  5.77 us
    ppermute x2, waiting for transfers between devices, padded_2(): lax.ppermute(lax.slice_in_dim(block, block.shape[dim] - width, None, axis...  5.37 us
  transfers between devices with their start and end apart: 4, of which 4 were waited for; matrix products, arithmetic and copies ran while one was open for 8% of the time, Pallas kernels for 0%

commit v1 on v0

v1 whole, which is shorter than its diff:
```python
import functools

import jax
import jax.numpy as jnp
from jax import lax
from jax.experimental import pallas as pl
from jax.experimental.pallas import tpu as pltpu
from jax.sharding import PartitionSpec as P

MESH = pl.DeviceIdType.MESH
LANES = 128


def permit(classes, permittivity):
    value = jnp.full(classes.shape, permittivity[0], jnp.float32)
    for index in range(1, permittivity.shape[0]):
        value = jnp.where(classes == index, permittivity[index], value)
    return value


def harmonic(first_value, second_value):
    return 2.0 * first_value * second_value / (first_value + second_value)


def split(value):
    high = value.astype(jnp.bfloat16)
    return high, (value - high.astype(jnp.float32)).astype(jnp.bfloat16)


def contract(left, right):
    return lax.dot_general(
        left, right, (((1,), (1,)), ((), ())), preferred_element_type=jnp.float32
    )


def store_split(target, row, value):
    rows = target.shape[0] // 2
    size = value.shape[0]
    high, low = split(value)
    target[row:row + size] = high
    target[rows + row:rows + row + size] = low


def fold(product):
    rows, columns = product.shape[0] // 2, product.shape[1] // 2
    return (
        product[:rows, :columns]
        + product[:rows, columns:]
        + product[rows:, :columns]
        + product[rows:, columns:]
    )


def kernel(
    nx, nz, v_hbm, c_hbm, permittivity, applied, coarse,
    v, c, eps, c_face, v_face, c_halo, v_halo,
    left_0, right_0, left_1, right_1, total, blocks, select, strip, rows,
    load_sem, c_send, c_recv, v_send, v_recv, strip_send, strip_recv,
):
    a, b = lax.axis_index("gx"), lax.axis_index("yz")
    count, cx, cz, ny = v.shape
    width = strip.shape[2]
    neighbour = ((a - 1, b), (a + 1, b), (a, b - 1), (a, b + 1))
    present = (a > 0, a < nx - 1, b > 0, b < nz - 1)

    load_c = pltpu.make_async_copy(c_hbm, c, load_sem.at[0])
    load_v = pltpu.make_async_copy(v_hbm, v, load_sem.at[1])
    load_c.start()
    load_v.start()

    barrier = pltpu.get_barrier_semaphore()
    for face in range(2):
        @pl.when(present[face])
        def _():
            pl.semaphore_signal(barrier, inc=1, device_id=neighbour[face], device_id_type=MESH)
    for step in range(1, nz):
        pl.semaphore_signal(
            barrier, inc=1, device_id=(a, lax.rem(b + step, nz)), device_id_type=MESH
        )
    partners = (a > 0).astype(jnp.int32) + (a < nx - 1).astype(jnp.int32) + (nz - 1)

    def copies(face, source, halo, send, recv):
        return pltpu.make_async_remote_copy(
            src_ref=source, dst_ref=halo.at[face ^ 1], send_sem=send.at[face],
            recv_sem=recv.at[face ^ 1], device_id=neighbour[face], device_id_type=MESH,
        )

    def arrival(face, source, halo, send, recv):
        return pltpu.make_async_remote_copy(
            src_ref=source, dst_ref=halo.at[face], send_sem=send.at[face],
            recv_sem=recv.at[face], device_id=neighbour[face], device_id_type=MESH,
        )

    ends = (0, cx - 1, 0, cz - 1)
    c_source = tuple(c_hbm.at[ends[f]] if f < 2 else c_face.at[f - 2] for f in range(4))
    v_source = tuple(v_hbm.at[:, ends[f]] if f < 2 else v_face.at[f - 2] for f in range(4))

    load_c.wait()
    for face in (2, 3):
        c_face[face - 2] = c[:, ends[face], :]
    load_v.wait()
    for face in (2, 3):
        for k in range(count):
            v_face[face - 2, k] = v[k, :, ends[face], :]

    pl.semaphore_wait(barrier, partners)
    for face in (2, 3, 0, 1):
        @pl.when(present[face])
        def _():
            copies(face, c_source[face], c_halo, c_send, c_recv).start()
    for face in (2, 3, 0, 1):
        @pl.when(present[face])
        def _():
            copies(face, v_source[face], v_halo, v_send, v_recv).start()

    for face in range(4):
        @pl.when(jnp.logical_not(present[face]))
        def _():
            c_halo[face] = jnp.zeros(c_halo.shape[1:], jnp.int32)
            v_halo[face] = jnp.zeros(v_halo.shape[1:], jnp.float32)

    for x in range(cx):
        eps[x] = permit(c[x], permittivity)
    total[...] = jnp.zeros_like(total)
    left_1[...] = jnp.zeros_like(left_1)
    right_1[...] = jnp.zeros_like(right_1)

    z_at = lax.broadcasted_iota(jnp.int32, (cz, ny), 0)
    y_at = lax.broadcasted_iota(jnp.int32, (cz, ny), 1)

    def plane(x, low_x, left, right):
        after = jnp.minimum(x + 1, cx - 1)
        before = jnp.maximum(x - 1, 0)
        own = eps[x]
        high_x = harmonic(own, eps[after]) * jnp.where(x < cx - 1, 1.0, 0.0)
        high_z = jnp.where(z_at < cz - 1, harmonic(own, pltpu.roll(own, cz - 1, 0)), 0.0)
        high_y = jnp.where(y_at < ny - 1, harmonic(own, pltpu.roll(own, ny - 1, 1)), 0.0)
        for k in range(count):
            value = v[k, x]
            flow_z = high_z * (value - pltpu.roll(value, cz - 1, 0))
            flow_y = high_y * (value - pltpu.roll(value, ny - 1, 1))
            result = high_x * (value - v[k, after]) + low_x * (value - v[k, before])
            result = result + (flow_z - pltpu.roll(flow_z, 1, 0))
            result = result + (flow_y - pltpu.roll(flow_y, 1, 1))
            applied[k, x] = result
            store_split(left, k * cz, value)
            store_split(right, k * cz, result)
        return high_x

    def pair(index, low_x):
        low_x = plane(2 * index, low_x, left_0, right_0)
        total[...] += contract(left_1[...], right_1[...])
        low_x = plane(2 * index + 1, low_x, left_1, right_1)
        total[...] += contract(left_0[...], right_0[...])
        return low_x

    lax.fori_loop(0, cx // 2, pair, jnp.zeros((cz, ny), jnp.float32))
    total[...] += contract(left_1[...], right_1[...])

    size = count * cz
    s = a * nz + b
    offsets = (0, -nz, nz, -1, 1)
    row = lax.broadcasted_iota(jnp.int32, (size, nz * width), 0) // cz
    column = lax.broadcasted_iota(jnp.int32, (size, nz * width), 1)
    inside = column % width
    target = (column // width) * (nx * count) + inside
    for j in range(5):
        hit = (target == (s + offsets[j]) * count + row) & (inside < nx * count)
        select[j * size:(j + 1) * size] = jnp.where(hit, 1.0, 0.0).astype(jnp.bfloat16)

    own_block = fold(total[...])
    for face in range(4):
        @pl.when(present[face])
        def _():
            arrival(face, c_source[face], c_halo, c_send, c_recv).wait_recv()
        end = ends[face]
        inner = eps[end] if face < 2 else eps[:, end, :]
        weight = harmonic(inner, permit(c_halo[face], permittivity))
        weight = weight * jnp.where(present[face], 1.0, 0.0)
        for k in range(count):
            value = v[k, end] if face < 2 else v_face[face - 2, k]
            weighted = weight * value
            store_split(left_0 if face % 2 == 0 else left_1, k * cz, weighted)
            store_split(right_0, k * cz, value)
            if face < 2:
                applied[k, end] += weighted
            else:
                applied[k, :, end, :] += weighted
        left = left_0 if face % 2 == 0 else left_1
        own_block = own_block + fold(contract(left[...], right_0[...]))

        @pl.when(present[face])
        def _():
            arrival(face, v_source[face], v_halo, v_send, v_recv).wait_recv()
        for k in range(count):
            store_split(right_1, k * cz, v_halo[face, k])
        blocks[:, (face + 1) * size:(face + 2) * size] = -fold(contract(left[...], right_1[...]))
    blocks[:, :size] = own_block

    same = (
        lax.broadcasted_iota(jnp.int32, blocks.shape, 0) % cz
        == lax.broadcasted_iota(jnp.int32, blocks.shape, 1) % cz
    )
    kept = jnp.where(same, blocks[...], 0.0).reshape(count, cz, blocks.shape[1])
    kept = jnp.sum(kept, axis=1) * (1.0 / (cz * ny))
    high = kept.astype(jnp.bfloat16)
    rest = kept - high.astype(jnp.float32)
    middle = rest.astype(jnp.bfloat16)
    low = (rest - middle.astype(jnp.float32)).astype(jnp.bfloat16)
    placed = sum(
        jnp.dot(part, select[...], preferred_element_type=jnp.float32)
        for part in (low, middle, high)
    )
    for tile in range(nz):
        strip[tile] = placed[:, tile * width:(tile + 1) * width]

    def send_strip(step):
        peer = lax.rem(b + step, nz)
        return pltpu.make_async_remote_copy(
            src_ref=strip.at[peer], dst_ref=rows.at[b], send_sem=strip_send.at[step],
            recv_sem=strip_recv.at[step], device_id=(a, peer), device_id_type=MESH,
        )

    for step in range(1, nz):
        send_strip(step).start()
    rows[b] = strip[b]
    for face in range(4):
        @pl.when(present[face])
        def _():
            copies(face, c_source[face], c_halo, c_send, c_recv).wait_send()
            copies(face, v_source[face], v_halo, v_send, v_recv).wait_send()
    for step in range(1, nz):
        send_strip(step).wait()
    for tile in range(nz):
        coarse[tile * count:(tile + 1) * count, :] = rows[tile, :, :nx * count]


def shards(nx, nz, vectors, classes, permittivity):
    count, cx, cz, ny = vectors.shape
    width = -(-nx * count // LANES) * LANES
    size = count * cz
    f32, i32, bf16 = jnp.float32, jnp.int32, jnp.bfloat16
    dma = pltpu.SemaphoreType.DMA
    return pl.pallas_call(
        functools.partial(kernel, nx, nz),
        out_shape=(
            jax.ShapeDtypeStruct(vectors.shape, f32),
            jax.ShapeDtypeStruct((nz * count, nx * count), f32),
        ),
        in_specs=[
            pl.BlockSpec(memory_space=pl.ANY),
            pl.BlockSpec(memory_space=pl.ANY),
            pl.BlockSpec(memory_space=pltpu.SMEM),
        ],
        out_specs=(
            pl.BlockSpec(memory_space=pltpu.VMEM),
            pl.BlockSpec(memory_space=pltpu.VMEM),
        ),
        scratch_shapes=[
            pltpu.VMEM(vectors.shape, f32),
            pltpu.VMEM(classes.shape, i32),
            pltpu.VMEM(classes.shape, f32),
            pltpu.VMEM((2, cx, ny), i32),
            pltpu.VMEM((2, count, cx, ny), f32),
            pltpu.VMEM((4, cz, ny), i32),
            pltpu.VMEM((4, count, cz, ny), f32),
            pltpu.VMEM((2 * size, ny), bf16),
            pltpu.VMEM((2 * size, ny), bf16),
            pltpu.VMEM((2 * size, ny), bf16),
            pltpu.VMEM((2 * size, ny), bf16),
            pltpu.VMEM((2 * size, 2 * size), f32),
            pltpu.VMEM((size, 5 * size), f32),
            pltpu.VMEM((5 * size, nz * width), bf16),
            pltpu.VMEM((nz, count, width), f32),
            pltpu.VMEM((nz, count, width), f32),
            dma((2,)), dma((4,)), dma((4,)), dma((4,)), dma((4,)), dma((nz,)), dma((nz,)),
        ],
        compiler_params=pltpu.CompilerParams(
            collective_id=0, has_side_effects=True, vmem_limit_bytes=56 * 2**20
        ),
        cost_estimate=pl.CostEstimate(
            flops=2 * 4 * size * size * cx * ny, bytes_accessed=9 * 2**20, transcendentals=0
        ),
    )(vectors, classes, permittivity)


def solution(mesh):
    return jax.shard_map(
        functools.partial(shards, mesh.shape["gx"], mesh.shape["yz"]),
        mesh=mesh,
        in_specs=(P(None, "gx", "yz", None), P("gx", "yz", None), P()),
        out_specs=(P(None, "gx", "yz", None), P("gx", "yz")),
        check_vma=False,
    )
```

time: 102 us -> 28.3 us (0.28)
  the two profiles are of different devices: /device:TPU:2 before, /device:TPU:0 now
where the time goes in v1:
time: 28.3 us; the launch traced here: 28.1 us
  Pallas kernels  21.8 us (77%)
  local copies, waits for them, and re-layouts  5.66 us (20%)
  between operations  0.65 us (2%)
    pallas_call x1, Pallas kernels, shards(): pl.pallas_call(functools.partial(kernel, nx, nz), out_shape=(jax.ShapeDty...  21.8 us
    unnamed x4, local copies, waits for them, and re-layouts  5.66 us

profile of v1, /device:TPU:0, one launch (start us, length us, event | category | flops | bytes accessed | tf_op | source)
XLA Modules:
  0.0 28.1 jit_solution(1687480518423161159)
XLA Ops:
  0.6 21.8 %shard_map.50 = (f32[8,16,16,512]{3,2,1,0:T(8,128)}, f32[32,64]{1,0:T(8,128)}) custom-call(f32[8,16,16,512]{3,2,1,0:T(8,128)} %v_hbm.1, s32[16,16,512]{2,1,0:T(8,128)} %c_hbm.1, f32[4]{0:T(128)} %permittivity.1), custom_call_target="tpu_custom_call" | custom-call | flops 1073741824 | bytes 9437184 | tf_op jit(solution)/shard_map/pallas_call | solution.py:244
  22.5 0.0 copy-start
  22.5 5.0 %copy.7 = f32[8,16,16,512]{3,2,1,0:T(8,128)} copy(f32[8,16,16,512]{3,2,1,0:T(8,128)} %get-tuple-element.4) | data formatting | bytes 8388608
  27.5 0.0 copy-done
  27.5 0.6 %copy.8 = f32[32,64]{1,0:T(8,128)} copy(f32[32,64]{1,0:T(8,128)S(1)} %copy-done) | data formatting | bytes 16384
Async XLA Ops:
  22.5 5.1 %copy-start = (f32[32,64]{1,0:T(8,128)S(1)}, f32[32,64]{1,0:T(8,128)}, u32[]{:S(2)}) copy-start(f32[32,64]{1,0:T(8,128)} %get-tuple-element.5) | copy-start | bytes 24580

commit v2 on v1

--- a/solution.py
+++ b/solution.py
@@ -55,7 +55,7 @@
     nx, nz, v_hbm, c_hbm, permittivity, applied, coarse,
     v, c, eps, c_face, v_face, c_halo, v_halo,
     left_0, right_0, left_1, right_1, total, blocks, select, strip, rows,
-    load_sem, c_send, c_recv, v_send, v_recv, strip_send, strip_recv,
+    face_sem, load_sem, c_send, c_recv, v_send, v_recv, strip_send, strip_recv,
 ):
     a, b = lax.axis_index("gx"), lax.axis_index("yz")
     count, cx, cz, ny = v.shape
@@ -63,10 +63,18 @@
     neighbour = ((a - 1, b), (a + 1, b), (a, b - 1), (a, b + 1))
     present = (a > 0, a < nx - 1, b > 0, b < nz - 1)
 
-    load_c = pltpu.make_async_copy(c_hbm, c, load_sem.at[0])
-    load_v = pltpu.make_async_copy(v_hbm, v, load_sem.at[1])
+    def load(index):
+        part = pl.ds(2 * index, 2)
+        return pltpu.make_async_copy(v_hbm.at[:, part], v.at[:, part], load_sem.at[index])
+
+    load_c = pltpu.make_async_copy(c_hbm, c, face_sem.at[0])
+    load_low = pltpu.make_async_copy(v_hbm.at[:, :, 0, :], v_face.at[0], face_sem.at[1])
+    load_high = pltpu.make_async_copy(v_hbm.at[:, :, cz - 1, :], v_face.at[1], face_sem.at[2])
     load_c.start()
-    load_v.start()
+    load_low.start()
+    load_high.start()
+    for index in range(cx // 2):
+        load(index).start()
 
     barrier = pltpu.get_barrier_semaphore()
     for face in range(2):
@@ -98,11 +106,8 @@
     load_c.wait()
     for face in (2, 3):
         c_face[face - 2] = c[:, ends[face], :]
-    load_v.wait()
-    for face in (2, 3):
-        for k in range(count):
-            v_face[face - 2, k] = v[k, :, ends[face], :]
-
+    load_low.wait()
+    load_high.wait()
     pl.semaphore_wait(barrier, partners)
     for face in (2, 3, 0, 1):
         @pl.when(present[face])
@@ -148,12 +153,16 @@
         return high_x
 
     def pair(index, low_x):
+        @pl.when(index < cx // 2 - 1)
+        def _():
+            load(index + 1).wait()
         low_x = plane(2 * index, low_x, left_0, right_0)
         total[...] += contract(left_1[...], right_1[...])
         low_x = plane(2 * index + 1, low_x, left_1, right_1)
         total[...] += contract(left_0[...], right_0[...])
         return low_x
 
+    load(0).wait()
     lax.fori_loop(0, cx // 2, pair, jnp.zeros((cz, ny), jnp.float32))
     total[...] += contract(left_1[...], right_1[...])
 
@@ -235,21 +244,32 @@
         coarse[tile * count:(tile + 1) * count, :] = rows[tile, :, :nx * count]
 
 
+def store(applied, coarse, applied_out, coarse_out, sem):
+    copies = (
+        pltpu.make_async_copy(applied, applied_out, sem.at[0]),
+        pltpu.make_async_copy(coarse, coarse_out, sem.at[1]),
+    )
+    for copy in copies:
+        copy.start()
+    for copy in copies:
+        copy.wait()
+
+
 def shards(nx, nz, vectors, classes, permittivity):
     count, cx, cz, ny = vectors.shape
     width = -(-nx * count // LANES) * LANES
     size = count * cz
     f32, i32, bf16 = jnp.float32, jnp.int32, jnp.bfloat16
     dma = pltpu.SemaphoreType.DMA
-    return pl.pallas_call(
+    results = pl.pallas_call(
         functools.partial(kernel, nx, nz),
         out_shape=(
             jax.ShapeDtypeStruct(vectors.shape, f32),
             jax.ShapeDtypeStruct((nz * count, nx * count), f32),
         ),
         in_specs=[
-            pl.BlockSpec(memory_space=pl.ANY),
-            pl.BlockSpec(memory_space=pl.ANY),
+            pl.BlockSpec(memory_space=pltpu.HBM),
+            pl.BlockSpec(memory_space=pltpu.HBM),
             pl.BlockSpec(memory_space=pltpu.SMEM),
         ],
         out_specs=(
@@ -273,15 +293,23 @@
             pltpu.VMEM((5 * size, nz * width), bf16),
             pltpu.VMEM((nz, count, width), f32),
             pltpu.VMEM((nz, count, width), f32),
-            dma((2,)), dma((4,)), dma((4,)), dma((4,)), dma((4,)), dma((nz,)), dma((nz,)),
+            dma((3,)), dma((cx // 2,)), dma((4,)), dma((4,)), dma((4,)), dma((4,)), dma((nz,)), dma((nz,)),
         ],
         compiler_params=pltpu.CompilerParams(
-            collective_id=0, has_side_effects=True, vmem_limit_bytes=56 * 2**20
+            collective_id=0, has_side_effects=True, vmem_limit_bytes=48 * 2**20
         ),
         cost_estimate=pl.CostEstimate(
             flops=2 * 4 * size * size * cx * ny, bytes_accessed=9 * 2**20, transcendentals=0
         ),
     )(vectors, classes, permittivity)
+    return pl.pallas_call(
+        store,
+        out_shape=tuple(jax.ShapeDtypeStruct(result.shape, f32) for result in results),
+        in_specs=[pl.BlockSpec(memory_space=pl.ANY)] * 2,
+        out_specs=(pl.BlockSpec(memory_space=pltpu.HBM),) * 2,
+        scratch_shapes=[dma((2,))],
+        cost_estimate=pl.CostEstimate(flops=0, bytes_accessed=8 * 2**20, transcendentals=0),
+    )(*results)
 
 
 def solution(mesh):

time: 28.3 us -> 153 us (5.41)
  Pallas kernels: 21.8 us -> 147 us
    pallas_call x0 -> x1, Pallas kernels: none -> 129 us  [shards(): pl.pallas_call(store, out_shape=tuple((jax.ShapeDtypeStruct(result.shape,...]
    pallas_call x1, Pallas kernels: 21.8 us -> 18.4 us  [shards(): pl.pallas_call(functools.partial(kernel, nx, nz), out_shape=(jax.ShapeDty...]
    unnamed x4 -> x8, local copies, waits for them, and re-layouts: 5.66 us -> 4.21 us
where the time goes in v2:
time: 153 us; the launch traced here: 152 us
  Pallas kernels  147 us (96%)
  local copies, waits for them, and re-layouts  4.21 us (3%)
    pallas_call x1, Pallas kernels, shards(): pl.pallas_call(store, out_shape=tuple((jax.ShapeDtypeStruct(result.shape,...  129 us
    pallas_call x1, Pallas kernels, shards(): pl.pallas_call(functools.partial(kernel, nx, nz), out_shape=(jax.ShapeDty...  18.4 us
    unnamed x8, local copies, waits for them, and re-layouts  4.21 us

profile of v2, /device:TPU:0, one launch (start us, length us, event | category | flops | bytes accessed | tf_op | source)
XLA Modules:
  0.0 151.9 jit_solution(3368953637880075738)
XLA Ops:
  0.6 0.0 copy-start.1
  0.6 1.0 copy-done.1
  1.7 0.0 copy-start.3
  1.7 0.7 copy-done.3
  2.3 18.4 %shard_map.50 = (f32[8,16,16,512]{3,2,1,0:T(8,128)S(1)}, f32[32,64]{1,0:T(8,128)S(1)}) custom-call(f32[8,16,16,512]{3,2,1,0:T(8,128)} %v_hbm.1, s32[16,16,512]{2,1,0:T(8,128)S(1)} %copy-done.1, f32[4]{0:T(128)S(1)} %copy-done.3), custom_call_target="tpu_custom_call" | custom-call | flops 1073741824 | bytes 9437184 | tf_op jit(solution)/shard_map/pallas_call | solution.py:264
  20.7 0.0 copy-start
  20.7 1.9 %copy-done = f32[8,16,16,512]{3,2,1,0:T(8,128)} copy-done((f32[8,16,16,512]{3,2,1,0:T(8,128)}, f32[8,16,16,512]{3,2,1,0:T(8,128)S(1)}, u32[]{:S(2)}) %copy-start) | copy-done | bytes 4194328
  22.7 0.0 copy-start.2
  22.7 0.6 copy-done.2
  23.3 128.7 %shard_map.51 = (f32[8,16,16,512]{3,2,1,0:T(8,128)}, f32[32,64]{1,0:T(8,128)}) custom-call(f32[8,16,16,512]{3,2,1,0:T(8,128)} %copy-done, f32[32,64]{1,0:T(8,128)} %copy-done.2), custom_call_target="tpu_custom_call" | custom-call | bytes 8388608 | tf_op jit(solution)/shard_map/pallas_call | solution.py:305
Async XLA Ops:
  0.6 1.0 copy-start.1
  1.7 0.7 copy-start.3
  20.7 1.9 %copy-start = (f32[8,16,16,512]{3,2,1,0:T(8,128)}, f32[8,16,16,512]{3,2,1,0:T(8,128)S(1)}, u32[]{:S(2)}) copy-start(f32[8,16,16,512]{3,2,1,0:T(8,128)S(1)} %get-tuple-element.4.applied) | copy-start | bytes 12582916
  22.7 0.6 copy-start.2

commit v3 on v2

--- a/solution.py
+++ b/solution.py
@@ -33,12 +33,13 @@
     )
 
 
-def store_split(target, row, value):
+def store_split(target, row, value, face=0):
     rows = target.shape[0] // 2
-    size = value.shape[0]
+    size, columns = value.shape
     high, low = split(value)
-    target[row:row + size] = high
-    target[rows + row:rows + row + size] = low
+    lanes = slice(face * columns, (face + 1) * columns)
+    target[row:row + size, lanes] = high
+    target[rows + row:rows + row + size, lanes] = low
 
 
 def fold(product):
@@ -54,7 +55,7 @@
 def kernel(
     nx, nz, v_hbm, c_hbm, permittivity, applied, coarse,
     v, c, eps, c_face, v_face, c_halo, v_halo,
-    left_0, right_0, left_1, right_1, total, blocks, select, strip, rows,
+    left_0, right_0, left_1, right_1, flow_x, left_f, own_f, halo_f, total, blocks, select, strip, rows,
     face_sem, load_sem, c_send, c_recv, v_send, v_recv, strip_send, strip_recv,
 ):
     a, b = lax.axis_index("gx"), lax.axis_index("yz")
@@ -133,9 +134,10 @@
     z_at = lax.broadcasted_iota(jnp.int32, (cz, ny), 0)
     y_at = lax.broadcasted_iota(jnp.int32, (cz, ny), 1)
 
-    def plane(x, low_x, left, right):
+    flow_x[...] = jnp.zeros_like(flow_x)
+
+    def plane(x, left, right):
         after = jnp.minimum(x + 1, cx - 1)
-        before = jnp.maximum(x - 1, 0)
         own = eps[x]
         high_x = harmonic(own, eps[after]) * jnp.where(x < cx - 1, 1.0, 0.0)
         high_z = jnp.where(z_at < cz - 1, harmonic(own, pltpu.roll(own, cz - 1, 0)), 0.0)
@@ -144,28 +146,27 @@
             value = v[k, x]
             flow_z = high_z * (value - pltpu.roll(value, cz - 1, 0))
             flow_y = high_y * (value - pltpu.roll(value, ny - 1, 1))
-            result = high_x * (value - v[k, after]) + low_x * (value - v[k, before])
+            flow = high_x * (value - v[k, after])
+            result = flow - flow_x[k]
+            flow_x[k] = flow
             result = result + (flow_z - pltpu.roll(flow_z, 1, 0))
             result = result + (flow_y - pltpu.roll(flow_y, 1, 1))
             applied[k, x] = result
             store_split(left, k * cz, value)
             store_split(right, k * cz, result)
-        return high_x
-
-    def pair(index, low_x):
+
+    def pair(index, carry):
         @pl.when(index < cx // 2 - 1)
         def _():
             load(index + 1).wait()
-        low_x = plane(2 * index, low_x, left_0, right_0)
+        plane(2 * index, left_0, right_0)
         total[...] += contract(left_1[...], right_1[...])
-        low_x = plane(2 * index + 1, low_x, left_1, right_1)
+        plane(2 * index + 1, left_1, right_1)
         total[...] += contract(left_0[...], right_0[...])
-        return low_x
+        return carry
 
     load(0).wait()
-    lax.fori_loop(0, cx // 2, pair, jnp.zeros((cz, ny), jnp.float32))
-    total[...] += contract(left_1[...], right_1[...])
-
+    lax.fori_loop(0, cx // 2, pair, 0)
     size = count * cz
     s = a * nz + b
     offsets = (0, -nz, nz, -1, 1)
@@ -177,11 +178,11 @@
         hit = (target == (s + offsets[j]) * count + row) & (inside < nx * count)
         select[j * size:(j + 1) * size] = jnp.where(hit, 1.0, 0.0).astype(jnp.bfloat16)
 
-    own_block = fold(total[...])
     for face in range(4):
         @pl.when(present[face])
         def _():
             arrival(face, c_source[face], c_halo, c_send, c_recv).wait_recv()
+    for face in range(4):
         end = ends[face]
         inner = eps[end] if face < 2 else eps[:, end, :]
         weight = harmonic(inner, permit(c_halo[face], permittivity))
@@ -189,21 +190,26 @@
         for k in range(count):
             value = v[k, end] if face < 2 else v_face[face - 2, k]
             weighted = weight * value
-            store_split(left_0 if face % 2 == 0 else left_1, k * cz, weighted)
-            store_split(right_0, k * cz, value)
+            store_split(left_f, k * cz, weighted, face)
+            store_split(own_f, k * cz, value, face)
             if face < 2:
                 applied[k, end] += weighted
             else:
                 applied[k, :, end, :] += weighted
-        left = left_0 if face % 2 == 0 else left_1
-        own_block = own_block + fold(contract(left[...], right_0[...]))
-
+    total[...] += contract(left_1[...], right_1[...])
+    own_block = fold(total[...] + contract(left_f[...], own_f[...]))
+
+    for face in range(4):
         @pl.when(present[face])
         def _():
             arrival(face, v_source[face], v_halo, v_send, v_recv).wait_recv()
+    for face in range(4):
+        lanes = slice(face * ny, (face + 1) * ny)
         for k in range(count):
-            store_split(right_1, k * cz, v_halo[face, k])
-        blocks[:, (face + 1) * size:(face + 2) * size] = -fold(contract(left[...], right_1[...]))
+            store_split(halo_f, k * cz, v_halo[face, k], face)
+        blocks[:, (face + 1) * size:(face + 2) * size] = -fold(
+            contract(left_f[:, lanes], halo_f[:, lanes])
+        )
     blocks[:, :size] = own_block
 
     same = (
@@ -212,14 +218,12 @@
     )
     kept = jnp.where(same, blocks[...], 0.0).reshape(count, cz, blocks.shape[1])
     kept = jnp.sum(kept, axis=1) * (1.0 / (cz * ny))
-    high = kept.astype(jnp.bfloat16)
-    rest = kept - high.astype(jnp.float32)
-    middle = rest.astype(jnp.bfloat16)
-    low = (rest - middle.astype(jnp.float32)).astype(jnp.bfloat16)
-    placed = sum(
-        jnp.dot(part, select[...], preferred_element_type=jnp.float32)
-        for part in (low, middle, high)
-    )
+    high = kept.astype(jnp.bfloat16).astype(jnp.float32)
+    rest = kept - high
+    middle = rest.astype(jnp.bfloat16).astype(jnp.float32)
+    parts = jnp.concatenate([rest - middle, middle, high], axis=0).astype(jnp.bfloat16)
+    placed = jnp.dot(parts, select[...], preferred_element_type=jnp.float32)
+    placed = placed[:count] + placed[count:2 * count] + placed[2 * count:]
     for tile in range(nz):
         strip[tile] = placed[:, tile * width:(tile + 1) * width]
 
@@ -288,6 +292,10 @@
             pltpu.VMEM((2 * size, ny), bf16),
             pltpu.VMEM((2 * size, ny), bf16),
             pltpu.VMEM((2 * size, ny), bf16),
+            pltpu.VMEM((count, cz, ny), f32),
+            pltpu.VMEM((2 * size, 4 * ny), bf16),
+            pltpu.VMEM((2 * size, 4 * ny), bf16),
+            pltpu.VMEM((2 * size, 4 * ny), bf16),
             pltpu.VMEM((2 * size, 2 * size), f32),
             pltpu.VMEM((size, 5 * size), f32),
             pltpu.VMEM((5 * size, nz * width), bf16),
@@ -305,8 +313,8 @@
     return pl.pallas_call(
         store,
         out_shape=tuple(jax.ShapeDtypeStruct(result.shape, f32) for result in results),
-        in_specs=[pl.BlockSpec(memory_space=pl.ANY)] * 2,
-        out_specs=(pl.BlockSpec(memory_space=pltpu.HBM),) * 2,
+        in_specs=[pl.BlockSpec(memory_space=pltpu.VMEM)] * 2,
+        out_specs=(pl.BlockSpec(memory_space=pl.ANY),) * 2,
         scratch_shapes=[dma((2,))],
         cost_estimate=pl.CostEstimate(flops=0, bytes_accessed=8 * 2**20, transcendentals=0),
     )(*results)

time: 153 us -> 27.1 us (0.18)
  Pallas kernels: 147 us -> 22.1 us
    pallas_call x1, Pallas kernels: 129 us -> 4.22 us  [shards(): pl.pallas_call(store, out_shape=tuple((jax.ShapeDtypeStruct(result.shape,...]
where the time goes in v3:
time: 27.1 us; the launch traced here: 26.9 us
  Pallas kernels  22.1 us (82%)
  local copies, waits for them, and re-layouts  4.21 us (16%)
  between operations  0.66 us (2%)
    pallas_call x1, Pallas kernels, shards(): pl.pallas_call(functools.partial(kernel, nx, nz), out_shape=(jax.ShapeDty...  17.8 us
    pallas_call x1, Pallas kernels, shards(): pl.pallas_call(store, out_shape=tuple((jax.ShapeDtypeStruct(result.shape,...  4.22 us
    unnamed x8, local copies, waits for them, and re-layouts  4.21 us

profile of v3, /device:TPU:0, one launch (start us, length us, event | category | flops | bytes accessed | tf_op | source)
XLA Modules:
  0.0 26.9 jit_solution(10100530335735390391)
XLA Ops:
  0.6 0.0 copy-start.1
  0.6 1.0 %copy-done.1 = s32[16,16,512]{2,1,0:T(8,128)S(1)} copy-done((s32[16,16,512]{2,1,0:T(8,128)S(1)}, s32[16,16,512]{2,1,0:T(8,128)}, u32[]{:S(2)}) %copy-start.1) | copy-done | bytes 524312
  1.7 0.0 copy-start.3
  1.7 0.7 %copy-done.3 = f32[4]{0:T(128)S(1)} copy-done((f32[4]{0:T(128)S(1)}, f32[4]{0:T(128)}, u32[]{:S(2)}) %copy-start.3) | copy-done | bytes 40
  2.3 17.8 %shard_map.50 = (f32[8,16,16,512]{3,2,1,0:T(8,128)S(1)}, f32[32,64]{1,0:T(8,128)S(1)}) custom-call(f32[8,16,16,512]{3,2,1,0:T(8,128)} %v_hbm.1, s32[16,16,512]{2,1,0:T(8,128)S(1)} %copy-done.1, f32[4]{0:T(128)S(1)} %copy-done.3), custom_call_target="tpu_custom_call" | custom-call | flops 1073741824 | bytes 9437184 | tf_op jit(solution)/shard_map/pallas_call | solution.py:268
  20.2 0.0 copy-start
  20.2 1.9 %copy-done = f32[8,16,16,512]{3,2,1,0:T(8,128)} copy-done((f32[8,16,16,512]{3,2,1,0:T(8,128)}, f32[8,16,16,512]{3,2,1,0:T(8,128)S(1)}, u32[]{:S(2)}) %copy-start) | copy-done | bytes 4194328
  22.1 0.0 copy-start.2
  22.1 0.6 %copy-done.2 = f32[32,64]{1,0:T(8,128)} copy-done((f32[32,64]{1,0:T(8,128)}, f32[32,64]{1,0:T(8,128)S(1)}, u32[]{:S(2)}) %copy-start.2) | copy-done | bytes 8216
  22.7 4.2 %shard_map.51 = (f32[8,16,16,512]{3,2,1,0:T(8,128)}, f32[32,64]{1,0:T(8,128)}) custom-call(f32[8,16,16,512]{3,2,1,0:T(8,128)} %copy-done, f32[32,64]{1,0:T(8,128)} %copy-done.2), custom_call_target="tpu_custom_call" | custom-call | bytes 8388608 | tf_op jit(solution)/shard_map/pallas_call | solution.py:313
Async XLA Ops:
  0.6 1.0 %copy-start.1 = (s32[16,16,512]{2,1,0:T(8,128)S(1)}, s32[16,16,512]{2,1,0:T(8,128)}, u32[]{:S(2)}) copy-start(s32[16,16,512]{2,1,0:T(8,128)} %c_hbm.1) | copy-start | bytes 1572868
  1.7 0.7 %copy-start.3 = (f32[4]{0:T(128)S(1)}, f32[4]{0:T(128)}, u32[]{:S(2)}) copy-start(f32[4]{0:T(128)} %permittivity.1) | copy-start | bytes 52
  20.2 1.9 %copy-start = (f32[8,16,16,512]{3,2,1,0:T(8,128)}, f32[8,16,16,512]{3,2,1,0:T(8,128)S(1)}, u32[]{:S(2)}) copy-start(f32[8,16,16,512]{3,2,1,0:T(8,128)S(1)} %get-tuple-element.4.applied) | copy-start | bytes 12582916
  22.1 0.6 %copy-start.2 = (f32[32,64]{1,0:T(8,128)}, f32[32,64]{1,0:T(8,128)S(1)}, u32[]{:S(2)}) copy-start(f32[32,64]{1,0:T(8,128)S(1)} %get-tuple-element.5.coarse) | copy-start | bytes 24580

commit v4 on v3

--- a/solution.py
+++ b/solution.py
@@ -248,24 +248,17 @@
         coarse[tile * count:(tile + 1) * count, :] = rows[tile, :, :nx * count]
 
 
-def store(applied, coarse, applied_out, coarse_out, sem):
-    copies = (
-        pltpu.make_async_copy(applied, applied_out, sem.at[0]),
-        pltpu.make_async_copy(coarse, coarse_out, sem.at[1]),
-    )
-    for copy in copies:
-        copy.start()
-    for copy in copies:
-        copy.wait()
-
-
 def shards(nx, nz, vectors, classes, permittivity):
     count, cx, cz, ny = vectors.shape
     width = -(-nx * count // LANES) * LANES
     size = count * cz
     f32, i32, bf16 = jnp.float32, jnp.int32, jnp.bfloat16
     dma = pltpu.SemaphoreType.DMA
-    results = pl.pallas_call(
+    vectors, classes, permittivity = (
+        pltpu.with_memory_space_constraint(array, pltpu.HBM)
+        for array in (vectors, classes, permittivity)
+    )
+    return pl.pallas_call(
         functools.partial(kernel, nx, nz),
         out_shape=(
             jax.ShapeDtypeStruct(vectors.shape, f32),
@@ -310,14 +303,6 @@
             flops=2 * 4 * size * size * cx * ny, bytes_accessed=9 * 2**20, transcendentals=0
         ),
     )(vectors, classes, permittivity)
-    return pl.pallas_call(
-        store,
-        out_shape=tuple(jax.ShapeDtypeStruct(result.shape, f32) for result in results),
-        in_specs=[pl.BlockSpec(memory_space=pltpu.VMEM)] * 2,
-        out_specs=(pl.BlockSpec(memory_space=pl.ANY),) * 2,
-        scratch_shapes=[dma((2,))],
-        cost_estimate=pl.CostEstimate(flops=0, bytes_accessed=8 * 2**20, transcendentals=0),
-    )(*results)
 
 
 def solution(mesh):

time: 27.1 us -> 21.4 us (0.79)
  Pallas kernels: 22.1 us -> 18 us
  local copies, waits for them, and re-layouts: 4.21 us -> 2.62 us
    pallas_call x1 -> x0, Pallas kernels: 4.22 us -> none  [shards(): pl.pallas_call(store, out_shape=tuple((jax.ShapeDtypeStruct(result.shape,...]
    unnamed x8 -> x2, local copies, waits for them, and re-layouts: 4.21 us -> 2.62 us
where the time goes in v4:
time: 21.4 us; the launch traced here: 21.2 us
  Pallas kernels  18 us (84%)
  local copies, waits for them, and re-layouts  2.62 us (12%)
  between operations  0.64 us (3%)
    pallas_call x1, Pallas kernels, shards(): pl.pallas_call(functools.partial(kernel, nx, nz), out_shape=(jax.ShapeDty...  18 us
    unnamed x2, local copies, waits for them, and re-layouts  2.62 us

profile of v4, /device:TPU:0, one launch (start us, length us, event | category | flops | bytes accessed | tf_op | source)
XLA Modules:
  0.0 21.2 jit_solution(5198288699491995440)
XLA Ops:
  0.6 18.0 %shard_map.50 = (f32[8,16,16,512]{3,2,1,0:T(8,128)S(1)}, f32[32,64]{1,0:T(8,128)S(1)}) custom-call(f32[8,16,16,512]{3,2,1,0:T(8,128)} %v_hbm.1, s32[16,16,512]{2,1,0:T(8,128)} %c_hbm.1, f32[4]{0:T(128)} %permittivity.1), custom_call_target="tpu_custom_call" | custom-call | flops 1073741824 | bytes 9437184 | tf_op jit(solution)/shard_map/pallas_call | solution.py:261
  18.6 2.0 %copy.7 = f32[8,16,16,512]{3,2,1,0:T(8,128)} copy(f32[8,16,16,512]{3,2,1,0:T(8,128)S(1)} %get-tuple-element.4) | data formatting | bytes 8388608
  20.6 0.6 %copy.8 = f32[32,64]{1,0:T(8,128)} copy(f32[32,64]{1,0:T(8,128)S(1)} %get-tuple-element.5) | data formatting | bytes 16384

commit v5 on v4

--- a/solution.py
+++ b/solution.py
@@ -104,9 +104,26 @@
     c_source = tuple(c_hbm.at[ends[f]] if f < 2 else c_face.at[f - 2] for f in range(4))
     v_source = tuple(v_hbm.at[:, ends[f]] if f < 2 else v_face.at[f - 2] for f in range(4))
 
+    size = count * cz
+    s = a * nz + b
+    offsets = (0, -nz, nz, -1, 1)
+    row = lax.broadcasted_iota(jnp.int32, (size, nz * width), 0) // cz
+    column = lax.broadcasted_iota(jnp.int32, (size, nz * width), 1)
+    inside = column % width
+    target = (column // width) * (nx * count) + inside
+    for j in range(5):
+        hit = (target == (s + offsets[j]) * count + row) & (inside < nx * count)
+        select[j * size:(j + 1) * size] = jnp.where(hit, 1.0, 0.0).astype(jnp.bfloat16)
+    total[...] = jnp.zeros_like(total)
+    left_1[...] = jnp.zeros_like(left_1)
+    right_1[...] = jnp.zeros_like(right_1)
+    flow_x[...] = jnp.zeros_like(flow_x)
+
     load_c.wait()
     for face in (2, 3):
         c_face[face - 2] = c[:, ends[face], :]
+    for x in range(cx):
+        eps[x] = permit(c[x], permittivity)
     load_low.wait()
     load_high.wait()
     pl.semaphore_wait(barrier, partners)
@@ -125,16 +142,8 @@
             c_halo[face] = jnp.zeros(c_halo.shape[1:], jnp.int32)
             v_halo[face] = jnp.zeros(v_halo.shape[1:], jnp.float32)
 
-    for x in range(cx):
-        eps[x] = permit(c[x], permittivity)
-    total[...] = jnp.zeros_like(total)
-    left_1[...] = jnp.zeros_like(left_1)
-    right_1[...] = jnp.zeros_like(right_1)
-
     z_at = lax.broadcasted_iota(jnp.int32, (cz, ny), 0)
     y_at = lax.broadcasted_iota(jnp.int32, (cz, ny), 1)
-
-    flow_x[...] = jnp.zeros_like(flow_x)
 
     def plane(x, left, right):
         after = jnp.minimum(x + 1, cx - 1)
@@ -167,17 +176,6 @@
 
     load(0).wait()
     lax.fori_loop(0, cx // 2, pair, 0)
-    size = count * cz
-    s = a * nz + b
-    offsets = (0, -nz, nz, -1, 1)
-    row = lax.broadcasted_iota(jnp.int32, (size, nz * width), 0) // cz
-    column = lax.broadcasted_iota(jnp.int32, (size, nz * width), 1)
-    inside = column % width
-    target = (column // width) * (nx * count) + inside
-    for j in range(5):
-        hit = (target == (s + offsets[j]) * count + row) & (inside < nx * count)
-        select[j * size:(j + 1) * size] = jnp.where(hit, 1.0, 0.0).astype(jnp.bfloat16)
-
     for face in range(4):
         @pl.when(present[face])
         def _():
@@ -199,17 +197,18 @@
     total[...] += contract(left_1[...], right_1[...])
     own_block = fold(total[...] + contract(left_f[...], own_f[...]))
 
-    for face in range(4):
-        @pl.when(present[face])
-        def _():
-            arrival(face, v_source[face], v_halo, v_send, v_recv).wait_recv()
-    for face in range(4):
-        lanes = slice(face * ny, (face + 1) * ny)
-        for k in range(count):
-            store_split(halo_f, k * cz, v_halo[face, k], face)
-        blocks[:, (face + 1) * size:(face + 2) * size] = -fold(
-            contract(left_f[:, lanes], halo_f[:, lanes])
-        )
+    for faces in ((0, 1), (2, 3)):
+        for face in faces:
+            @pl.when(present[face])
+            def _():
+                arrival(face, v_source[face], v_halo, v_send, v_recv).wait_recv()
+        for face in faces:
+            lanes = slice(face * ny, (face + 1) * ny)
+            for k in range(count):
+                store_split(halo_f, k * cz, v_halo[face, k], face)
+            blocks[:, (face + 1) * size:(face + 2) * size] = -fold(
+                contract(left_f[:, lanes], halo_f[:, lanes])
+            )
     blocks[:, :size] = own_block
 
     same = (

time: 21.4 us -> 21.2 us (level)
  Pallas kernels: 18 us -> 17.7 us
where the time goes in v5:
time: 21.2 us; the launch traced here: 21 us
  Pallas kernels  17.7 us (83%)
  local copies, waits for them, and re-layouts  2.62 us (12%)
  between operations  0.64 us (3%)
    pallas_call x1, Pallas kernels, shards(): pl.pallas_call(functools.partial(kernel, nx, nz), out_shape=(jax.ShapeDty...  17.7 us
    unnamed x2, local copies, waits for them, and re-layouts  2.62 us

profile of v5, /device:TPU:0, one launch (start us, length us, event | category | flops | bytes accessed | tf_op | source)
XLA Modules:
  0.0 21.0 jit_solution(3409035092985840535)
XLA Ops:
  0.6 17.7 %shard_map.50 = (f32[8,16,16,512]{3,2,1,0:T(8,128)S(1)}, f32[32,64]{1,0:T(8,128)S(1)}) custom-call(f32[8,16,16,512]{3,2,1,0:T(8,128)} %v_hbm.1, s32[16,16,512]{2,1,0:T(8,128)} %c_hbm.1, f32[4]{0:T(128)} %permittivity.1), custom_call_target="tpu_custom_call" | custom-call | flops 1073741824 | bytes 9437184 | tf_op jit(solution)/shard_map/pallas_call | solution.py:260
  18.4 2.0 %copy.7 = f32[8,16,16,512]{3,2,1,0:T(8,128)} copy(f32[8,16,16,512]{3,2,1,0:T(8,128)S(1)} %get-tuple-element.4) | data formatting | bytes 8388608
  20.4 0.6 %copy.8 = f32[32,64]{1,0:T(8,128)} copy(f32[32,64]{1,0:T(8,128)S(1)} %get-tuple-element.5) | data formatting | bytes 16384

commit v6 on v5

--- a/solution.py
+++ b/solution.py
@@ -122,20 +122,22 @@
     load_c.wait()
     for face in (2, 3):
         c_face[face - 2] = c[:, ends[face], :]
+    pl.semaphore_wait(barrier, partners)
+    for face in (2, 3, 0, 1):
+        @pl.when(present[face])
+        def _():
+            copies(face, c_source[face], c_halo, c_send, c_recv).start()
+    load_low.wait()
+    for face in (2, 3, 0, 1):
+        if face == 3:
+            load_high.wait()
+
+        @pl.when(present[face])
+        def _():
+            copies(face, v_source[face], v_halo, v_send, v_recv).start()
+
     for x in range(cx):
         eps[x] = permit(c[x], permittivity)
-    load_low.wait()
-    load_high.wait()
-    pl.semaphore_wait(barrier, partners)
-    for face in (2, 3, 0, 1):
-        @pl.when(present[face])
-        def _():
-            copies(face, c_source[face], c_halo, c_send, c_recv).start()
-    for face in (2, 3, 0, 1):
-        @pl.when(present[face])
-        def _():
-            copies(face, v_source[face], v_halo, v_send, v_recv).start()
-
     for face in range(4):
         @pl.when(jnp.logical_not(present[face]))
         def _():

time: 21.2 us -> 21.2 us (level)
  no operation moved by 1% of the time
where the time goes in v6:
time: 21.2 us; the launch traced here: 21 us
  Pallas kernels  17.7 us (83%)
  local copies, waits for them, and re-layouts  2.62 us (12%)
  between operations  0.64 us (3%)
    pallas_call x1, Pallas kernels, shards(): pl.pallas_call(functools.partial(kernel, nx, nz), out_shape=(jax.ShapeDty...  17.7 us
    unnamed x2, local copies, waits for them, and re-layouts  2.62 us

profile of v6, /device:TPU:0, one launch (start us, length us, event | category | flops | bytes accessed | tf_op | source)
XLA Modules:
  0.0 21.0 jit_solution(12273398808504094755)
XLA Ops:
  0.6 17.7 %shard_map.50 = (f32[8,16,16,512]{3,2,1,0:T(8,128)S(1)}, f32[32,64]{1,0:T(8,128)S(1)}) custom-call(f32[8,16,16,512]{3,2,1,0:T(8,128)} %v_hbm.1, s32[16,16,512]{2,1,0:T(8,128)} %c_hbm.1, f32[4]{0:T(128)} %permittivity.1), custom_call_target="tpu_custom_call" | custom-call | flops 1073741824 | bytes 9437184 | tf_op jit(solution)/shard_map/pallas_call | solution.py:262
  18.4 2.0 %copy.7 = f32[8,16,16,512]{3,2,1,0:T(8,128)} copy(f32[8,16,16,512]{3,2,1,0:T(8,128)S(1)} %get-tuple-element.4) | data formatting | bytes 8388608
  20.4 0.6 %copy.8 = f32[32,64]{1,0:T(8,128)} copy(f32[32,64]{1,0:T(8,128)S(1)} %get-tuple-element.5) | data formatting | bytes 16384
